TPU v7x, 32 devices: a whole 2x2x4 slice. The times are simulated.
32 devices in a mesh: groups: 2 (over x), atom: 16 (over z, y, core).
Axes of the slice: x: 2, y: 2, z: 4, core: 2. Of those that a mesh axis runs over, the one named last changes fastest.
Arguments:
- factors: bfloat16 [128, 128, 6144], P(('groups', 'atom')), parts along dimension 0, may hold values from -6 to 6
- block_sizes: int32 [128], P(('groups', 'atom')), parts along dimension 0, may hold values from 1 to 128, 6144 in all
- trial_vectors: bfloat16 [128, 128, 128], P(('groups', 'atom')), parts along dimension 0, may hold values from -0.5 to 0.5
- pair_list: int32 [2048, 2], P(('groups', 'atom')), parts along dimension 0, may hold values from 0 to 63, as said below
Outputs:
- kblocks: bfloat16 [2048, 128, 128], P(('groups', 'atom')), parts along dimension 0
- sigma: bfloat16 [128, 128, 128], P(('groups', 'atom')), parts along dimension 0
There are 2 independent parts, one for each index of `groups`. A program takes and returns all parts, laid end to end along the dimension named above; each array names one. Nothing has to cross between parts.
Inputs may be any that keep to these rules, and one draw needn't show every extreme that they name: `pair_list`: the first block of each pair belongs to the owner whose rows hold the pair (pair p on owner p // 64, blocks a on owner a // 4); the second block's owner is that owner or up to 2 owners after it, never past the last. Pairs may repeat. `block_sizes`: their sum over a cluster is 6144.
All inputs are finite; a program needn't handle non-finite values. No bound on the sum of `block_sizes` on one device may be relied on, other than what follows from the above.
Results may differ from a plain program's by a relative error of at most 0.005.
Values may be sent and summed in bfloat16 or wider, within the bound.
A program may use at most 128 MiB of HBM per device.

v0:
```python
import math

import jax
import jax.numpy as jnp
from jax import lax
from jax.sharding import PartitionSpec as P

REACH = 2


def passed_along(value, axis, by):
    devices = lax.axis_size(axis)
    pairs = [(i, i + by) for i in range(devices) if 0 <= i + by < devices]
    return lax.ppermute(value, axis, pairs)


def on_device(factors, block_sizes, trial_vectors, pair_list):
    count = factors.shape[0]
    width = factors.shape[1]
    scale = 1.0 / math.sqrt(factors.shape[2])
    rows = lax.broadcasted_iota(jnp.int32, (count, width), 1)
    keep = (rows < block_sizes[:, None]).astype(factors.dtype)
    masked = factors * keep[:, :, None]
    pieces = [(masked, trial_vectors)]
    for step in range(1, REACH + 1):
        pieces.append(passed_along((masked, trial_vectors), "atom", -step))
    window_factors = jnp.concatenate([piece[0] for piece in pieces], axis=0)
    window_vectors = jnp.concatenate([piece[1] for piece in pieces], axis=0)
    slots = window_factors.shape[0]
    gram = jnp.einsum("aiq,bjq->abij", masked, window_factors, preferred_element_type=jnp.float32)
    gram_half = (gram * scale).astype(jnp.bfloat16)
    start = lax.axis_index("atom") * count
    local_first = pair_list[:, 0] - start
    local_second = pair_list[:, 1] - start
    different = (pair_list[:, 0] != pair_list[:, 1]).astype(jnp.float32)
    npairs = pair_list.shape[0]
    first_hot = (local_first[:, None] == jnp.arange(count, dtype=jnp.int32)[None, :]).astype(
        jnp.float32
    )
    second_hot = (local_second[:, None] == jnp.arange(slots, dtype=jnp.int32)[None, :]).astype(
        jnp.float32
    )
    pair_hot = first_hot[:, :, None] * second_hot[:, None, :]
    select = pair_hot.reshape(npairs, count * slots).astype(jnp.bfloat16)
    picked = jnp.dot(
        select, gram_half.reshape(count * slots, width * width), preferred_element_type=jnp.float32
    )
    kblocks = picked.astype(jnp.bfloat16).reshape(npairs, width, width)
    pair_count = jnp.sum(pair_hot, axis=0)
    cross_count = jnp.sum(pair_hot * different[:, None, None], axis=0)
    forward = jnp.einsum(
        "abij,bjk->abik", gram_half, window_vectors, preferred_element_type=jnp.float32
    )
    backward = jnp.einsum(
        "abij,aik->abjk", gram_half, trial_vectors, preferred_element_type=jnp.float32
    )
    own_terms = jnp.sum(pair_count[:, :, None, None] * forward, axis=1)
    slot_terms = jnp.sum(cross_count[:, :, None, None] * backward, axis=0)
    total = own_terms + slot_terms[0:count]
    for step in range(1, REACH + 1):
        total = total + passed_along(slot_terms[step * count : (step + 1) * count], "atom", step)
    return (kblocks, total.astype(jnp.bfloat16))


def solution(mesh):
    return jax.shard_map(
        on_device,
        mesh=mesh,
        in_specs=(
            P(("groups", "atom"), None, None),
            P(("groups", "atom")),
            P(("groups", "atom"), None, None),
            P(("groups", "atom"), None),
        ),
        out_specs=(P(("groups", "atom"), None, None), P(("groups", "atom"), None, None)),
        check_vma=False,
    )
```

profile of v0, /device:TPU:8, one launch (start us, length us, event | category | flops | bytes accessed | tf_op | source)
XLA Modules:
  0.0 252.1 jit_solution(10305325589612413963)
XLA Ops:
  0.6 0.7 fusion.23
  1.4 0.0 copy-start.3
  1.4 0.0 copy-start.5
  1.4 5.9 %broadcast_multiply_fusion = bf16[4,128,6144]{2,1,0:T(8,128)(2,1)} fusion(bf16[4,128,6144]{2,1,0:T(8,128)(2,1)} %param.4, bf16[4,128]{1,0:T(4,128)(2,1)S(1)} %fusion.23), kind=kLoop, calls=%fused_computation.12 | loop fusion | flops 3145728 | bytes 12583936 | tf_op jit(solution)/shard_map/mul | solution.py:23
  7.3 2.7 %collective-permute-start = (bf16[4,128,6144]{2,1,0:T(8,128)(2,1)}, bf16[4,128,6144]{2,1,0:T(8,128)(2,1)}, u32[]{:S(2)}, u32[]{:S(2)}) collective-permute-start(bf16[4,128,6144]{2,1,0:T(8,128)(2,1)} %broadcast_multiply_fusion), channel_id=1, source_target_pairs={{1,0},{2,1},{3,2},{4,3},{5,4},{6,5},{7,6},{8,7},{9,8},{10,9},{11,1... | collective-permute-start | bytes 18874376 | tf_op jit(solution)/shard_map/ppermute | solution.py:14
  10.0 2.5 collective-permute-start.1
  12.5 0.0 copy-done.3
  12.5 0.1 copy.29
  12.7 2.0 collective-permute-start.2
  14.7 1.9 collective-permute-start.3
  16.6 0.0 copy-done.5
  16.7 0.1 multiply_reduce_fusion.1
  16.8 0.7 copy.26
  17.5 126.6 %collective-permute-done = bf16[4,128,6144]{2,1,0:T(8,128)(2,1)} collective-permute-done((bf16[4,128,6144]{2,1,0:T(8,128)(2,1)}, bf16[4,128,6144]{2,1,0:T(8,128)(2,1)}, u32[]{:S(2)}, u32[]{:S(2)}) %collective-permute-start) | collective-permute-done | bytes 6291488 | tf_op jit(solution)/shard_map/ppermute | solution.py:14
  144.2 72.0 %collective-permute-done.1 = bf16[4,128,6144]{2,1,0:T(8,128)(2,1)} collective-permute-done((bf16[4,128,6144]{2,1,0:T(8,128)(2,1)}, bf16[4,128,6144]{2,1,0:T(8,128)(2,1)}, u32[]{:S(2)}, u32[]{:S(2)}) %collective-permute-start.1) | collective-permute-done | bytes 6291488 | tf_op jit(solution)/shard_map/ppermute | solution.py:14
  216.2 14.8 %fusion.12 = bf16[4,12,128,128]{2,3,0,1:T(8,128)(2,1)S(1)} fusion(bf16[4,128,6144]{2,1,0:T(8,128)(2,1)} %broadcast_multiply_fusion, bf16[4,128,6144]{2,1,0:T(8,128)(2,1)} %collective-permute-done.1, bf16[4,128,6144]{2,1,0:T(8,128)(2,1)} %collective-permute-done), kind=kOutput, calls=%fused_computation.16 | convolution fusion | flops 9721872384 | bytes 20447232 | tf_op jit(solution)/shard_map/aiq,bjq->abij/dot_general | solution.py:30
  231.1 0.0 copy-start.1
  231.1 0.9 copy.25
  232.0 0.0 copy-start
  232.0 0.8 multiply_reduce_fusion
  232.8 0.8 fusion.27
  233.6 1.8 copy.41
  235.4 1.9 collective-permute-start.4
  237.3 1.8 copy.42
  239.1 0.0 copy-done.1
  239.1 4.2 %collective-permute-start.5 = (f32[4,128,128]{1,2,0:T(8,128)}, f32[4,128,128]{1,2,0:T(8,128)}, u32[]{:S(2)}, u32[]{:S(2)}) collective-permute-start(f32[4,128,128]{1,2,0:T(8,128)} %copy.42), channel_id=1, source_target_pairs={{0,2},{1,3},{2,4},{3,5},{4,6},{5,7},{6,8},{7,9},{8,10},{9,11},{10,... | collective-permute-start | bytes 786440 | tf_op jit(solution)/shard_map/ppermute | solution.py:14
  243.4 0.0 copy-done
  243.4 0.0 copy-start.4
  243.4 2.8 %fusion.9 = bf16[8,8,128,128]{3,1,2,0:T(8,128)(2,1)S(1)} fusion(bf16[64,48]{0,1:T(8,128)(2,1)S(1)} %convert_element_type.58, bf16[6,8,128,128]{3,2,1,0:T(8,128)(2,1)} %bitcast.51), kind=kOutput, calls=%fused_computation.13 | convolution fusion | flops 101711872 | bytes 3676160 | tf_op jit(solution)/shard_map/dot_general | solution.py:45
  246.2 0.1 copy.40
  246.3 0.0 copy-start.2
  246.3 1.9 copy.44
  248.2 0.0 collective-permute-done.2
  248.2 0.0 collective-permute-done.3
  248.2 0.0 copy-done.4
  248.2 0.0 copy-done.2
  248.3 1.6 fusion.6
  249.8 0.0 collective-permute-done.4
  249.8 0.4 collective-permute-done.5
  250.2 1.1 add_convert_fusion
  251.3 0.8 copy.35
  (5 shorter events, 0.0 us)
Async XLA Ops:
  1.4 11.2 %copy-start.3 = (bf16[4,128,128]{2,1,0:T(8,128)(2,1)S(1)}, bf16[4,128,128]{2,1,0:T(8,128)(2,1)}, u32[]{:S(2)}) copy-start(bf16[4,128,128]{2,1,0:T(8,128)(2,1)} %param.6) | copy-start | bytes 393220
  1.4 15.3 %copy-start.5 = (s32[64,2]{0,1:T(2,128)S(1)}, s32[64,2]{0,1:T(2,128)}, u32[]{:S(2)}) copy-start(s32[64,2]{0,1:T(2,128)} %param.7) | copy-start | bytes 1540
  7.3 136.9 %collective-permute-start = (bf16[4,128,6144]{2,1,0:T(8,128)(2,1)}, bf16[4,128,6144]{2,1,0:T(8,128)(2,1)}, u32[]{:S(2)}, u32[]{:S(2)}) collective-permute-start(bf16[4,128,6144]{2,1,0:T(8,128)(2,1)} %broadcast_multiply_fusion), channel_id=1, source_target_pairs={{1,0},{2,1},{3,2},{4,3},{5,4},{6,5},{7,6},{8,7},{9,8},{10,9},{11,1... | collective-permute-start | bytes 18874376 | tf_op jit(solution)/shard_map/ppermute | solution.py:14
  10.0 206.2 %collective-permute-start.1 = (bf16[4,128,6144]{2,1,0:T(8,128)(2,1)}, bf16[4,128,6144]{2,1,0:T(8,128)(2,1)}, u32[]{:S(2)}, u32[]{:S(2)}) collective-permute-start(bf16[4,128,6144]{2,1,0:T(8,128)(2,1)} %broadcast_multiply_fusion), channel_id=1, source_target_pairs={{2,0},{3,1},{4,2},{5,3},{6,4},{7,5},{8,6},{9,7},{10,8},{11,9},{12,... | collective-permute-start | bytes 18874376 | tf_op jit(solution)/shard_map/ppermute | solution.py:14
  12.7 235.6 %collective-permute-start.2 = (bf16[4,128,128]{1,2,0:T(8,128)(2,1)S(1)}, bf16[4,128,128]{1,2,0:T(8,128)(2,1)}, u32[]{:S(2)}, u32[]{:S(2)}) collective-permute-start(bf16[4,128,128]{1,2,0:T(8,128)(2,1)S(1)} %copy.29), channel_id=1, source_target_pairs={{1,0},{2,1},{3,2},{4,3},{5,4},{6,5},{7,6},{8,7},{9,8},{10,9},{11,1... | collective-permute-start | bytes 393224 | tf_op jit(solution)/shard_map/ppermute | solution.py:14
  14.7 233.5 %collective-permute-start.3 = (bf16[4,128,128]{1,2,0:T(8,128)(2,1)S(1)}, bf16[4,128,128]{1,2,0:T(8,128)(2,1)}, u32[]{:S(2)}, u32[]{:S(2)}) collective-permute-start(bf16[4,128,128]{1,2,0:T(8,128)(2,1)S(1)} %copy.29), channel_id=1, source_target_pairs={{2,0},{3,1},{4,2},{5,3},{6,4},{7,5},{8,6},{9,7},{10,8},{11,9},{12,... | collective-permute-start | bytes 393224 | tf_op jit(solution)/shard_map/ppermute | solution.py:14
  231.1 8.1 %copy-start.1 = (bf16[4,12,128,128]{2,3,0,1:T(8,128)(2,1)}, bf16[4,12,128,128]{2,3,0,1:T(8,128)(2,1)S(1)}, u32[]{:S(2)}) copy-start(bf16[4,12,128,128]{2,3,0,1:T(8,128)(2,1)S(1)} %fusion.12) | copy-start | bytes 4718596
  232.0 11.4 %copy-start = (bf16[4,12,128,128]{3,2,1,0:T(8,128)(2,1)}, bf16[4,12,128,128]{3,2,1,0:T(8,128)(2,1)S(1)}, u32[]{:S(2)}) copy-start(bf16[4,12,128,128]{3,2,1,0:T(8,128)(2,1)S(1)} %copy.25) | copy-start | bytes 4718596
  235.4 14.4 %collective-permute-start.4 = (f32[4,128,128]{1,2,0:T(8,128)}, f32[4,128,128]{1,2,0:T(8,128)}, u32[]{:S(2)}, u32[]{:S(2)}) collective-permute-start(f32[4,128,128]{1,2,0:T(8,128)} %copy.41), channel_id=1, source_target_pairs={{0,1},{1,2},{2,3},{3,4},{4,5},{5,6},{6,7},{7,8},{8,9},{9,10},{10,1... | collective-permute-start | bytes 786440 | tf_op jit(solution)/shard_map/ppermute | solution.py:14
  239.1 11.1 %collective-permute-start.5 = (f32[4,128,128]{1,2,0:T(8,128)}, f32[4,128,128]{1,2,0:T(8,128)}, u32[]{:S(2)}, u32[]{:S(2)}) collective-permute-start(f32[4,128,128]{1,2,0:T(8,128)} %copy.42), channel_id=1, source_target_pairs={{0,2},{1,3},{2,4},{3,5},{4,6},{5,7},{6,8},{7,9},{8,10},{9,11},{10,... | collective-permute-start | bytes 786440 | tf_op jit(solution)/shard_map/ppermute | solution.py:14
  243.4 4.8 %copy-start.4 = (f32[4,12]{0,1:T(8,128)S(1)}, f32[4,12]{0,1:T(8,128)}, u32[]{:S(2)}) copy-start(f32[4,12]{0,1:T(8,128)} %copy.26) | copy-start | bytes 580
  246.3 1.9 copy-start.2
where the time goes:
time: 254 us; the launch traced here: 252 us
  waiting for transfers between devices  199 us (78%)
  matrix products  19.9 us (8%)
  starting transfers between devices  15.3 us (6%)
  local copies, waits for them, and re-layouts  9.01 us (4%)
  other arithmetic  7.88 us (3%)
    ppermute x6, waiting for transfers between devices, passed_along(): return lax.ppermute(value, axis, pairs)  199 us
    ppermute x6, starting transfers between devices, passed_along(): return lax.ppermute(value, axis, pairs)  15.3 us
    dot_general x1, matrix products, on_device(): jnp.einsum('aiq,bjq->abij', masked, window_factors, preferred_element_typ...  14.8 us
    unnamed x18, local copies, waits for them, and re-layouts  6.56 us
    mul x1, other arithmetic, on_device(): masked = factors * keep[:, :, None]  5.93 us
  transfers between devices with their start and end apart: 6, of which 3 were waited for; matrix products, arithmetic and copies ran while one was open for 11% of the time, Pallas kernels for 0%

commit v1 on v0

v1 whole, which is shorter than its diff:
```python
import math

import jax
import jax.numpy as jnp
from jax import lax
from jax.sharding import PartitionSpec as P

REACH = 2
CHUNKS = 2


def side(i):
    return (i // 2) % 2


def moved(value, pairs):
    return lax.ppermute(value, "atom", pairs)


def times(left, right):
    return lax.dot_general(left, right, (((1,), (1,)), ((), ())), preferred_element_type=jnp.float32)


def on_device(factors, block_sizes, trial_vectors, pair_list):
    count, width, depth = factors.shape
    rows = count * width
    half = depth // 2
    scale = 1.0 / math.sqrt(depth)
    devices = lax.axis_size("atom")
    ring = range(devices)
    me = lax.axis_index("atom")
    y = (me // 2) % 2
    core = me % 2
    bf16 = jnp.bfloat16

    flat = factors.reshape(rows, depth)
    keep = lax.dynamic_slice_in_dim(flat, y * half, half, 1)
    other = lax.dynamic_slice_in_dim(flat, (1 - y) * half, half, 1)

    step = rows // CHUNKS
    swap = [(i, i ^ 2) for i in ring]
    peers = [moved(other[j * step : (j + 1) * step], swap) for j in range(CHUNKS)]
    far = [(i, i - 4) for i in ring if side(i) == 0 and i >= 4]
    far += [(i, i + 4) for i in ring if side(i) == 1 and i + 4 < devices]
    outer = moved(keep, far)
    right = moved(flat, [(i, i - 1) for i in ring if i % 2 == 1])
    own_cross = moved(keep, [(i, i + 1) for i in ring if side(i) == 1 and i % 2 == 0])
    right_keep = lax.dynamic_slice_in_dim(right, y * half, half, 1)
    early = jnp.where(y == core, jnp.where(core == 0, right_keep, own_cross), jnp.zeros((), bf16))
    late = moved(
        outer,
        [(i, i + 1) for i in ring if side(i) == 0 and i % 2 == 0]
        + [(i, i - 1) for i in ring if side(i) == 1 and i % 2 == 1],
    )

    vectors, sizes = [trial_vectors], [block_sizes]
    for by in range(1, REACH + 1):
        back = [(i, i - by) for i in ring if i - by >= 0]
        vectors.append(moved(trial_vectors, back))
        sizes.append(moved(block_sizes, back))
    window_vectors = jnp.concatenate(vectors, axis=0)
    window_sizes = jnp.concatenate(sizes, axis=0)

    gram_own = times(flat, flat) * scale
    gram_right = times(flat, right) * scale

    natural, turned, cross_natural, cross_turned = [], [], [], []
    for peer in peers:
        with_own = times(peer, keep) * scale
        with_outer = times(peer, outer) * scale
        with_cross = (times(peer, early) + times(peer, late)) * scale
        natural.append(moved(jnp.where(y == 0, with_outer, with_own).astype(bf16), swap))
        from_far = moved(
            with_outer.astype(bf16), [(i, i - 4) for i in ring if side(i) == 1 and i >= 4]
        )
        turned.append(jnp.where(y == 0, with_own, from_far.astype(jnp.float32)))
        cross = with_cross.astype(bf16)
        cross_natural.append(moved(cross, [(i, i ^ 2) for i in ring if i % 2 == 1]))
        cross_turned.append(
            moved(
                cross,
                [(i, i + 1) for i in ring if i % 4 == 0]
                + [(i, i - 3) for i in ring if i % 4 == 2 and i >= 3],
            )
        )

    def joined(pieces):
        return jnp.concatenate(pieces, axis=0).astype(jnp.float32)

    gram_two = joined(natural) + joined(turned).T
    gram_odd = joined(cross_natural) + joined(cross_turned).T
    gram_one = jnp.where(core == 0, gram_right, gram_odd)
    gram = jnp.concatenate([gram_own, gram_one, gram_two], axis=1)

    slots = (REACH + 1) * count
    place = jnp.arange(width, dtype=jnp.int32)
    row_real = (place[None, :] < block_sizes[:, None]).reshape(rows, 1)
    column_real = (place[None, :] < window_sizes[:, None]).reshape(1, slots * width)
    gram = jnp.where(row_real & column_real, gram, 0.0).astype(bf16)
    gram_half = gram.reshape(count, width, slots, width).transpose(0, 2, 1, 3)

    start = me * count
    local_first = pair_list[:, 0] - start
    local_second = pair_list[:, 1] - start
    different = (pair_list[:, 0] != pair_list[:, 1]).astype(jnp.float32)
    npairs = pair_list.shape[0]
    first_hot = (local_first[:, None] == jnp.arange(count, dtype=jnp.int32)[None, :]).astype(
        jnp.float32
    )
    second_hot = (local_second[:, None] == jnp.arange(slots, dtype=jnp.int32)[None, :]).astype(
        jnp.float32
    )
    pair_hot = first_hot[:, :, None] * second_hot[:, None, :]
    select = pair_hot.reshape(npairs, count * slots).astype(bf16)
    picked = jnp.dot(
        select, gram_half.reshape(count * slots, width * width), preferred_element_type=jnp.float32
    )
    kblocks = picked.astype(bf16).reshape(npairs, width, width)
    pair_count = jnp.sum(pair_hot, axis=0)
    cross_count = jnp.sum(pair_hot * different[:, None, None], axis=0)
    forward = jnp.einsum(
        "abij,bjk->abik", gram_half, window_vectors, preferred_element_type=jnp.float32
    )
    backward = jnp.einsum(
        "abij,aik->abjk", gram_half, trial_vectors, preferred_element_type=jnp.float32
    )
    own_terms = jnp.sum(pair_count[:, :, None, None] * forward, axis=1)
    slot_terms = jnp.sum(cross_count[:, :, None, None] * backward, axis=0)
    total = own_terms + slot_terms[0:count]
    for by in range(1, REACH + 1):
        ahead = [(i, i + by) for i in ring if i + by < devices]
        total = total + moved(slot_terms[by * count : (by + 1) * count], ahead)
    return (kblocks, total.astype(bf16))


def solution(mesh):
    return jax.shard_map(
        on_device,
        mesh=mesh,
        in_specs=(
            P(("groups", "atom"), None, None),
            P(("groups", "atom")),
            P(("groups", "atom"), None, None),
            P(("groups", "atom"), None),
        ),
        out_specs=(P(("groups", "atom"), None, None), P(("groups", "atom"), None, None)),
        check_vma=False,
    )
```

time: 254 us -> 187 us (0.74)
  waiting for transfers between devices: 199 us -> 64.1 us
  starting transfers between devices: 15.3 us -> 53.9 us
  matrix products: 19.9 us -> 45.5 us
  local copies, waits for them, and re-layouts: 9.01 us -> 17.9 us
  other arithmetic: 7.88 us -> 4.3 us
    ppermute x6 -> x20, waiting for transfers between devices: 199 us -> 64.1 us  [moved(): return lax.ppermute(value, 'atom', pairs)]
    ppermute x6 -> x20, starting transfers between devices: 15.3 us -> 53.9 us  [moved(): return lax.ppermute(value, 'atom', pairs)]
    dot_general x1 -> x10, matrix products: 14.8 us -> 41.6 us  [times(): lax.dot_general(left, right, (((1,), (1,)), ((), ())), preferred_element_...]
    mul x1 -> x0, other arithmetic: 5.93 us -> none  [on_device(): masked = factors * keep[:, :, None]]
    dynamic_slice x0 -> x1, local copies, waits for them, and re-layouts: none -> 3.73 us  [on_device(): keep = lax.dynamic_slice_in_dim(flat, y * half, half, 1)]
    unnamed x18 -> x22, local copies, waits for them, and re-layouts: 6.56 us -> 8.13 us
  transfers between devices with their start and end apart: 6 -> 20, of which waited for: 3 -> 6; matrix products, arithmetic and copies ran while one was open for 11% -> 36% of each run, Pallas kernels for 0% -> 0%
where the time goes in v1:
time: 187 us
  waiting for transfers between devices  64.1 us (34%)
  starting transfers between devices  53.9 us (29%)
  matrix products  45.5 us (24%)
  local copies, waits for them, and re-layouts  17.9 us (10%)
  other arithmetic  4.3 us (2%)
    ppermute x20, waiting for transfers between devices, moved(): return lax.ppermute(value, 'atom', pairs)  64.1 us
    ppermute x20, starting transfers between devices, moved(): return lax.ppermute(value, 'atom', pairs)  53.9 us
    dot_general x10, matrix products, times(): lax.dot_general(left, right, (((1,), (1,)), ((), ())), preferred_element_...  41.6 us
    unnamed x22, local copies, waits for them, and re-layouts  8.13 us
  transfers between devices with their start and end apart: 20, of which 6 were waited for; matrix products, arithmetic and copies ran while one was open for 36% of the time, Pallas kernels for 0%

profile of v1, /device:TPU:8, one launch (start us, length us, event | category | flops | bytes accessed | tf_op | source)
XLA Modules:
  0.0 186.7 jit_solution(2673218879757644839)
XLA Ops:
  0.6 1.3 collective-permute-start.2
  2.0 3.7 %constant_dynamic-slice_fusion.1 = bf16[512,3072]{1,0:T(8,128)(2,1)} fusion(bf16[512,6144]{1,0:T(8,128)(2,1)} %bitcast.68, s32[]{:T(128)S(6)} %select_n.78), kind=kLoop, calls=%fused_computation.54 | loop fusion | bytes 6291460 | tf_op jit(solution)/shard_map/dynamic_slice | solution.py:37
  5.7 1.9 %collective-permute-start.5 = (bf16[512,3072]{1,0:T(8,128)(2,1)}, bf16[512,3072]{1,0:T(8,128)(2,1)}, u32[]{:S(2)}, u32[]{:S(2)}) collective-permute-start(bf16[512,3072]{1,0:T(8,128)(2,1)} %constant_dynamic-slice_fusion.1), channel_id=1, source_target_pairs={{4,0},{5,1},{8,4},{9,5},{12,8},{13,9},{2,6},{3,7},{6,10},{7,11},{1... | collective-permute-start | bytes 9437192 | tf_op jit(solution)/shard_map/ppermute | solution.py:17
  7.6 2.4 %collective-permute-start.4 = (bf16[512,3072]{1,0:T(8,128)(2,1)}, bf16[512,3072]{1,0:T(8,128)(2,1)}, u32[]{:S(2)}, u32[]{:S(2)}) collective-permute-start(bf16[512,3072]{1,0:T(8,128)(2,1)} %constant_dynamic-slice_fusion.1), channel_id=1, source_target_pairs={{2,3},{6,7},{10,11},{14,15},{18,19},{22,23},{26,27},{30,31}} | collective-permute-start | bytes 9437192 | tf_op jit(solution)/shard_map/ppermute | solution.py:17
  10.0 2.2 %constant_dynamic-slice_fusion = (bf16[256,3072]{1,0:T(8,128)(2,1)S(1)}, bf16[256,3072]{1,0:T(8,128)(2,1)S(1)}) fusion(bf16[512,6144]{1,0:T(8,128)(2,1)} %bitcast.69, s32[]{:T(128)S(6)} %select_n.75, s32[]{:T(128)S(6)} %add.49), kind=kLoop, calls=%fused_computation.53 | loop fusion | bytes 6291464 | tf_op jit(solution)/shard_map/slice | solution.py:42
  12.2 7.9 %collective-permute-start.3 = (bf16[256,3072]{1,0:T(8,128)(2,1)S(1)}, bf16[256,3072]{1,0:T(8,128)(2,1)}, u32[]{:S(2)}, u32[]{:S(2)}) collective-permute-start(bf16[256,3072]{1,0:T(8,128)(2,1)S(1)} %get-tuple-element.8), channel_id=1, source_target_pairs={{0,2},{1,3},{2,0},{3,1},{4,6},{5,7},{6,4},{7,5},{8,10},{9,11},{10,... | collective-permute-start | bytes 4718600 | tf_op jit(solution)/shard_map/ppermute | solution.py:17
  20.1 0.1 collective-permute-start.8
  20.2 4.2 %convolution_multiply_fusion.1 = bf16[512,512]{0,1:T(8,128)(2,1)} fusion(bf16[512,6144]{1,0:T(8,128)(2,1)S(1)} %bitcast.71), kind=kOutput, calls=%fused_computation.12 | convolution fusion | flops 3221749760 | bytes 6815744 | tf_op jit(solution)/shard_map/dot_general | solution.py:21
  24.5 0.7 multiply_reduce_fusion.1
  25.2 50.9 %collective-permute-done.5 = bf16[512,3072]{1,0:T(8,128)(2,1)} collective-permute-done((bf16[512,3072]{1,0:T(8,128)(2,1)}, bf16[512,3072]{1,0:T(8,128)(2,1)}, u32[]{:S(2)}, u32[]{:S(2)}) %collective-permute-start.5) | collective-permute-done | bytes 3145760 | tf_op jit(solution)/shard_map/ppermute | solution.py:17
  76.0 6.5 %collective-permute-start.6 = (bf16[512,3072]{1,0:T(8,128)(2,1)}, bf16[512,3072]{1,0:T(8,128)(2,1)}, u32[]{:S(2)}, u32[]{:S(2)}) collective-permute-start(bf16[512,3072]{1,0:T(8,128)(2,1)} %collective-permute-done.5), channel_id=1, source_target_pairs={{0,1},{4,5},{8,9},{12,13},{3,2},{7,6},{11,10},{15,14},{16,17},{20,... | collective-permute-start | bytes 9437192 | tf_op jit(solution)/shard_map/ppermute | solution.py:17
  82.6 0.5 iota_compare_fusion.2
  83.1 0.7 copy.50
  83.8 0.8 copy.53
  84.6 1.6 collective-permute-done.8
  86.2 1.9 %collective-permute-start = (s32[4]{0:T(128)S(1)}, s32[4]{0:T(128)S(1)}, u32[]{:S(2)}, u32[]{:S(2)}) collective-permute-start(s32[4]{0:T(128)S(1)} %copy-done.7), channel_id=1, source_target_pairs={{1,0},{2,1},{3,2},{4,3},{5,4},{6,5},{7,6},{8,7},{9,8},{10,9},{11,1... | collective-permute-start | bytes 56 | tf_op jit(solution)/shard_map/ppermute | solution.py:17
  88.1 3.4 %convolution_multiply_fusion.2 = f32[256,512]{1,0:T(8,128)S(1)} fusion(bf16[256,3072]{1,0:T(8,128)(2,1)} %collective-permute-done.8, bf16[512,3072]{1,0:T(8,128)(2,1)} %constant_dynamic-slice_fusion.1), kind=kOutput, calls=%fused_computation.14 | convolution fusion | flops 805437440 | bytes 5242880 | tf_op jit(solution)/shard_map/dot_general | solution.py:21
  91.5 3.4 %convolution_multiply_fusion.4 = f32[256,512]{1,0:T(8,128)S(1)} fusion(bf16[256,3072]{1,0:T(8,128)(2,1)} %collective-permute-done.3, bf16[512,3072]{1,0:T(8,128)(2,1)} %constant_dynamic-slice_fusion.1), kind=kOutput, calls=%fused_computation.16 | convolution fusion | flops 805437440 | bytes 5242880 | tf_op jit(solution)/shard_map/dot_general | solution.py:21
  94.9 4.1 %select_convert_fusion.1 = (bf16[256,512]{1,0:T(8,128)(2,1)S(1)}, bf16[256,512]{1,0:T(8,128)(2,1)}) fusion(f32[256,512]{1,0:T(8,128)S(1)} %convolution_multiply_fusion.2, pred[]{:T(512)S(6)} %eq.61, bf16[256,3072]{1,0:T(8,128)(2,1)} %collective-permute-done.8, bf16[512,3072]{1,0:T(8,128)(2,1)} %collective-permute-done.5), kind=kOutput, calls=%fused_computation.30 | convolution fusion | flops 805699584 | bytes 5767169 | tf_op jit(solution)/shard_map/dot_general | solution.py:21
  98.9 1.7 collective-permute-start.13
  100.7 4.1 %select_convert_fusion.2 = (bf16[256,512]{1,0:T(8,128)(2,1)S(1)}, bf16[256,512]{1,0:T(8,128)(2,1)}) fusion(f32[256,512]{1,0:T(8,128)S(1)} %convolution_multiply_fusion.4, pred[]{:T(512)S(6)} %eq.61, bf16[256,3072]{1,0:T(8,128)(2,1)} %collective-permute-done.3, bf16[512,3072]{1,0:T(8,128)(2,1)} %collective-permute-done.5), kind=kOutput, calls=%fused_computation.31 | convolution fusion | flops 805699584 | bytes 5767169 | tf_op jit(solution)/shard_map/dot_general | solution.py:21
  104.8 3.5 %collective-permute-start.1 = (s32[4]{0:T(128)S(1)}, s32[4]{0:T(128)S(1)}, u32[]{:S(2)}, u32[]{:S(2)}) collective-permute-start(s32[4]{0:T(128)S(1)} %copy-done.7), channel_id=1, source_target_pairs={{2,0},{3,1},{4,2},{5,3},{6,4},{7,5},{8,6},{9,7},{10,8},{11,9},{12,... | collective-permute-start | bytes 56 | tf_op jit(solution)/shard_map/ppermute | solution.py:17
  108.2 2.0 %collective-permute-done.1 = s32[4]{0:T(128)S(1)} collective-permute-done((s32[4]{0:T(128)S(1)}, s32[4]{0:T(128)S(1)}, u32[]{:S(2)}, u32[]{:S(2)}) %collective-permute-start.1) | collective-permute-done | bytes 48 | tf_op jit(solution)/shard_map/ppermute | solution.py:17
  110.2 1.2 collective-permute-start.12
  111.4 0.1 pad_add_fusion
  111.5 0.7 collective-permute-start.15
  112.1 0.1 iota_compare_fusion
  112.2 5.3 %collective-permute-done.12 = bf16[256,512]{1,0:T(8,128)(2,1)S(1)} collective-permute-done((bf16[256,512]{1,0:T(8,128)(2,1)S(1)}, bf16[256,512]{1,0:T(8,128)(2,1)S(1)}, u32[]{:S(2)}, u32[]{:S(2)}) %collective-permute-start.12) | collective-permute-done | bytes 262176 | tf_op jit(solution)/shard_map/ppermute | solution.py:17
  117.5 1.4 collective-permute-start.14
  118.9 0.1 maximum_convert_fusion
  119.0 0.3 copy.48
  119.3 5.5 %collective-permute-start.17 = (bf16[4,128,128]{1,2,0:T(8,128)(2,1)}, bf16[4,128,128]{1,2,0:T(8,128)(2,1)}, u32[]{:S(2)}, u32[]{:S(2)}) collective-permute-start(bf16[4,128,128]{1,2,0:T(8,128)(2,1)} %copy.53), channel_id=1, source_target_pairs={{2,0},{3,1},{4,2},{5,3},{6,4},{7,5},{8,6},{9,7},{10,8},{11,9},{12,... | collective-permute-start | bytes 393224 | tf_op jit(solution)/shard_map/ppermute | solution.py:17
  124.8 0.1 convert_select_fusion
  124.9 1.0 convert_select_fusion.1
  126.0 3.4 %fusion.11 = f32[256,512]{1,0:T(8,128)S(1)} fusion(bf16[256,3072]{1,0:T(8,128)(2,1)} %collective-permute-done.8, bf16[512,3072]{1,0:T(8,128)(2,1)} %collective-permute-done.4, bf16[512,6144]{1,0:T(8,128)(2,1)} %collective-permute-done.2, s32[]{:T(128)S(6)} %select_n.78, pred[]{:T(512)S(6)} %eq.59, pred[]{:T(512)S(6)} %eq.60), kind=kOutput, calls=%fused_computation.32 | convolution fusion | flops 808452096 | bytes 8388614 | tf_op jit(solution)/shard_map/dot_general | solution.py:21
  129.4 3.4 %fusion.9 = bf16[256,512]{1,0:T(8,128)(2,1)S(1)} fusion(f32[256,512]{1,0:T(8,128)S(1)} %fusion.11, bf16[256,3072]{1,0:T(8,128)(2,1)} %collective-permute-done.8, bf16[512,3072]{1,0:T(8,128)(2,1)} %collective-permute-done.6), kind=kOutput, calls=%fused_computation.23 | convolution fusion | flops 805699584 | bytes 5505024 | tf_op jit(solution)/shard_map/dot_general | solution.py:21
  132.8 0.1 copy.46
  132.9 2.0 %collective-permute-start.11 = (bf16[256,512]{1,0:T(8,128)(2,1)S(1)}, bf16[256,512]{1,0:T(8,128)(2,1)}, u32[]{:S(2)}, u32[]{:S(2)}) collective-permute-start(bf16[256,512]{1,0:T(8,128)(2,1)S(1)} %fusion.9), channel_id=1, source_target_pairs={{0,1},{4,5},{8,9},{12,13},{6,3},{10,7},{14,11},{16,17},{20,21},{24... | collective-permute-start | bytes 786440 | tf_op jit(solution)/shard_map/ppermute | solution.py:17
  134.9 3.4 %fusion.12 = f32[256,512]{0,1:T(8,128)S(1)} fusion(bf16[256,3072]{1,0:T(8,128)(2,1)} %collective-permute-done.3, bf16[512,3072]{1,0:T(8,128)(2,1)} %collective-permute-done.4, bf16[512,6144]{1,0:T(8,128)(2,1)} %collective-permute-done.2, s32[]{:T(128)S(6)} %select_n.78, pred[]{:T(512)S(6)} %eq.59, pred[]{:T(512)S(6)} %eq.60), kind=kOutput, calls=%fused_computation.33 | convolution fusion | flops 808452096 | bytes 8388614 | tf_op jit(solution)/shard_map/dot_general | solution.py:21
  138.3 4.1 %fusion.8 = bf16[256,512]{0,1:T(8,128)(2,1)} fusion(f32[256,512]{0,1:T(8,128)S(1)} %fusion.12, bf16[256,3072]{1,0:T(8,128)(2,1)} %collective-permute-done.3, bf16[512,3072]{1,0:T(8,128)(2,1)} %collective-permute-done.6), kind=kOutput, calls=%fused_computation.22 | convolution fusion | flops 805699584 | bytes 5505024 | tf_op jit(solution)/shard_map/dot_general | solution.py:21
  142.4 1.3 collective-permute-start.10
  143.7 1.4 collective-permute-start.7
  145.1 1.4 collective-permute-start.9
  146.5 0.3 fusion.10
  146.7 8.1 %collective-permute-start.16 = (bf16[4,128,128]{1,2,0:T(8,128)(2,1)}, bf16[4,128,128]{1,2,0:T(8,128)(2,1)}, u32[]{:S(2)}, u32[]{:S(2)}) collective-permute-start(bf16[4,128,128]{1,2,0:T(8,128)(2,1)} %copy.53), channel_id=1, source_target_pairs={{1,0},{2,1},{3,2},{4,3},{5,4},{6,5},{7,6},{8,7},{9,8},{10,9},{11,1... | collective-permute-start | bytes 393224 | tf_op jit(solution)/shard_map/ppermute | solution.py:17
  154.9 0.1 copy.47
  155.0 8.2 %fusion.5 = bf16[512,512]{0,1:T(8,128)(2,1)S(1)} fusion(bf16[512,6144]{1,0:T(8,128)(2,1)} %bitcast.70, bf16[512,6144]{1,0:T(8,128)(2,1)} %collective-permute-done.2, bf16[256,512]{0,1:T(8,128)(2,1)} %collective-permute-done.9, bf16[256,512]{0,1:T(8,128)(2,1)} %collective-permute-done.7, bf16[256,512]{1,0:T(8,128)(2,1)} %collective-permute-done.11, ...), kind=kOutput, calls=%fused_computation.13 | convolution fusion | flops 3224109056 | bytes 14155777 | tf_op jit(solution)/shard_map/dot_general | solution.py:21
  163.3 0.1 pad_maximum_fusion
  163.4 0.4 concatenate.29
  163.8 1.2 copy.49
  165.0 1.3 select_convert_fusion
  166.3 0.8 multiply_reduce_fusion
  167.0 0.9 fusion.28
  167.9 1.1 copy.65
  169.0 1.8 copy.66
  170.8 1.8 copy.67
  172.6 1.9 %collective-permute-start.19 = (f32[4,128,128]{1,2,0:T(8,128)}, f32[4,128,128]{1,2,0:T(8,128)S(1)}, u32[]{:S(2)}, u32[]{:S(2)}) collective-permute-start(f32[4,128,128]{1,2,0:T(8,128)} %copy.67), channel_id=1, source_target_pairs={{0,2},{1,3},{2,4},{3,5},{4,6},{5,7},{6,8},{7,9},{8,10},{9,11},{10,... | collective-permute-start | bytes 786440 | tf_op jit(solution)/shard_map/ppermute | solution.py:17
  174.5 1.9 %collective-permute-start.18 = (f32[4,128,128]{1,2,0:T(8,128)}, f32[4,128,128]{1,2,0:T(8,128)S(1)}, u32[]{:S(2)}, u32[]{:S(2)}) collective-permute-start(f32[4,128,128]{1,2,0:T(8,128)} %copy.66), channel_id=1, source_target_pairs={{0,1},{1,2},{2,3},{3,4},{4,5},{5,6},{6,7},{7,8},{8,9},{9,10},{10,1... | collective-permute-start | bytes 786440 | tf_op jit(solution)/shard_map/ppermute | solution.py:17
  176.5 1.4 fusion.1
  177.8 1.9 %copy.69 = bf16[8,8,128,128]{3,2,1,0:T(8,128)(2,1)} copy(bf16[8,8,128,128]{3,1,2,0:T(8,128)(2,1)S(1)} %fusion.1) | data formatting | bytes 4194304
  179.7 1.8 fusion
  181.5 3.3 %collective-permute-done.19 = f32[4,128,128]{1,2,0:T(8,128)S(1)} collective-permute-done((f32[4,128,128]{1,2,0:T(8,128)}, f32[4,128,128]{1,2,0:T(8,128)S(1)}, u32[]{:S(2)}, u32[]{:S(2)}) %collective-permute-start.19) | collective-permute-done | bytes 262176 | tf_op jit(solution)/shard_map/ppermute | solution.py:17
  184.8 1.0 collective-permute-done.18
  185.9 0.8 copy.59
  (36 shorter events, 0.2 us)
Async XLA Ops:
  0.6 125.3 %collective-permute-start.2 = (bf16[512,6144]{1,0:T(8,128)(2,1)}, bf16[512,6144]{1,0:T(8,128)(2,1)}, u32[]{:S(2)}, u32[]{:S(2)}) collective-permute-start(bf16[512,6144]{1,0:T(8,128)(2,1)} %bitcast.67), channel_id=1, source_target_pairs={{1,0},{3,2},{5,4},{7,6},{9,8},{11,10},{13,12},{15,14},{17,16},{19,... | collective-permute-start | bytes 18874376 | tf_op jit(solution)/shard_map/ppermute | solution.py:17
  5.7 70.3 %collective-permute-start.5 = (bf16[512,3072]{1,0:T(8,128)(2,1)}, bf16[512,3072]{1,0:T(8,128)(2,1)}, u32[]{:S(2)}, u32[]{:S(2)}) collective-permute-start(bf16[512,3072]{1,0:T(8,128)(2,1)} %constant_dynamic-slice_fusion.1), channel_id=1, source_target_pairs={{4,0},{5,1},{8,4},{9,5},{12,8},{13,9},{2,6},{3,7},{6,10},{7,11},{1... | collective-permute-start | bytes 9437192 | tf_op jit(solution)/shard_map/ppermute | solution.py:17
  7.6 118.3 %collective-permute-start.4 = (bf16[512,3072]{1,0:T(8,128)(2,1)}, bf16[512,3072]{1,0:T(8,128)(2,1)}, u32[]{:S(2)}, u32[]{:S(2)}) collective-permute-start(bf16[512,3072]{1,0:T(8,128)(2,1)} %constant_dynamic-slice_fusion.1), channel_id=1, source_target_pairs={{2,3},{6,7},{10,11},{14,15},{18,19},{22,23},{26,27},{30,31}} | collective-permute-start | bytes 9437192 | tf_op jit(solution)/shard_map/ppermute | solution.py:17
  10.0 10.2 %copy-start = (bf16[4,128,6144]{2,1,0:T(8,128)(2,1)S(1)}, bf16[4,128,6144]{2,1,0:T(8,128)(2,1)}, u32[]{:S(2)}) copy-start(bf16[4,128,6144]{2,1,0:T(8,128)(2,1)} %param.4) | copy-start | bytes 18874372
  12.2 79.2 %collective-permute-start.3 = (bf16[256,3072]{1,0:T(8,128)(2,1)S(1)}, bf16[256,3072]{1,0:T(8,128)(2,1)}, u32[]{:S(2)}, u32[]{:S(2)}) collective-permute-start(bf16[256,3072]{1,0:T(8,128)(2,1)S(1)} %get-tuple-element.8), channel_id=1, source_target_pairs={{0,2},{1,3},{2,0},{3,1},{4,6},{5,7},{6,4},{7,5},{8,10},{9,11},{10,... | collective-permute-start | bytes 4718600 | tf_op jit(solution)/shard_map/ppermute | solution.py:17
  20.1 4.4 %copy-start.5 = (s32[64,2]{0,1:T(2,128)S(1)}, s32[64,2]{0,1:T(2,128)}, u32[]{:S(2)}) copy-start(s32[64,2]{0,1:T(2,128)} %param.7) | copy-start | bytes 1540
  20.1 62.5 %copy-start.7 = (s32[4]{0:T(128)S(1)}, s32[4]{0:T(128)}, u32[]{:S(2)}) copy-start(s32[4]{0:T(128)} %param.5) | copy-start | bytes 52
  20.1 63.7 %copy-start.2 = (bf16[4,128,128]{2,1,0:T(8,128)(2,1)S(1)}, bf16[4,128,128]{2,1,0:T(8,128)(2,1)}, u32[]{:S(2)}) copy-start(bf16[4,128,128]{2,1,0:T(8,128)(2,1)} %param.6) | copy-start | bytes 393220
  20.1 66.1 %collective-permute-start.8 = (bf16[256,3072]{1,0:T(8,128)(2,1)S(1)}, bf16[256,3072]{1,0:T(8,128)(2,1)}, u32[]{:S(2)}, u32[]{:S(2)}) collective-permute-start(bf16[256,3072]{1,0:T(8,128)(2,1)S(1)} %get-tuple-element.9), channel_id=1, source_target_pairs={{0,2},{1,3},{2,0},{3,1},{4,6},{5,7},{6,4},{7,5},{8,10},{9,11},{10,... | collective-permute-start | bytes 4718600 | tf_op jit(solution)/shard_map/ppermute | solution.py:17
  76.0 53.3 %collective-permute-start.6 = (bf16[512,3072]{1,0:T(8,128)(2,1)}, bf16[512,3072]{1,0:T(8,128)(2,1)}, u32[]{:S(2)}, u32[]{:S(2)}) collective-permute-start(bf16[512,3072]{1,0:T(8,128)(2,1)} %collective-permute-done.5), channel_id=1, source_target_pairs={{0,1},{4,5},{8,9},{12,13},{3,2},{7,6},{11,10},{15,14},{16,17},{20,... | collective-permute-start | bytes 9437192 | tf_op jit(solution)/shard_map/ppermute | solution.py:17
  86.2 18.6 %collective-permute-start = (s32[4]{0:T(128)S(1)}, s32[4]{0:T(128)S(1)}, u32[]{:S(2)}, u32[]{:S(2)}) collective-permute-start(s32[4]{0:T(128)S(1)} %copy-done.7), channel_id=1, source_target_pairs={{1,0},{2,1},{3,2},{4,3},{5,4},{6,5},{7,6},{8,7},{9,8},{10,9},{11,1... | collective-permute-start | bytes 56 | tf_op jit(solution)/shard_map/ppermute | solution.py:17
  98.9 12.5 %collective-permute-start.13 = (bf16[256,512]{1,0:T(8,128)(2,1)S(1)}, bf16[256,512]{1,0:T(8,128)(2,1)S(1)}, u32[]{:S(2)}, u32[]{:S(2)}) collective-permute-start(bf16[256,512]{1,0:T(8,128)(2,1)S(1)} %get-tuple-element.16), channel_id=1, source_target_pairs={{0,2},{1,3},{2,0},{3,1},{4,6},{5,7},{6,4},{7,5},{8,10},{9,11},{10,... | collective-permute-start | bytes 786440 | tf_op jit(solution)/shard_map/ppermute | solution.py:17
  104.8 5.4 %collective-permute-start.1 = (s32[4]{0:T(128)S(1)}, s32[4]{0:T(128)S(1)}, u32[]{:S(2)}, u32[]{:S(2)}) collective-permute-start(s32[4]{0:T(128)S(1)} %copy-done.7), channel_id=1, source_target_pairs={{2,0},{3,1},{4,2},{5,3},{6,4},{7,5},{8,6},{9,7},{10,8},{11,9},{12,... | collective-permute-start | bytes 56 | tf_op jit(solution)/shard_map/ppermute | solution.py:17
  110.2 7.3 %collective-permute-start.12 = (bf16[256,512]{1,0:T(8,128)(2,1)S(1)}, bf16[256,512]{1,0:T(8,128)(2,1)S(1)}, u32[]{:S(2)}, u32[]{:S(2)}) collective-permute-start(bf16[256,512]{1,0:T(8,128)(2,1)S(1)} %get-tuple-element.18), channel_id=1, source_target_pairs={{0,2},{1,3},{2,0},{3,1},{4,6},{5,7},{6,4},{7,5},{8,10},{9,11},{10,... | collective-permute-start | bytes 786440 | tf_op jit(solution)/shard_map/ppermute | solution.py:17
  111.5 7.9 %collective-permute-start.15 = (bf16[256,512]{1,0:T(8,128)(2,1)}, bf16[256,512]{1,0:T(8,128)(2,1)S(1)}, u32[]{:S(2)}, u32[]{:S(2)}) collective-permute-start(bf16[256,512]{1,0:T(8,128)(2,1)} %get-tuple-element.17), channel_id=1, source_target_pairs={{6,2},{7,3},{10,6},{11,7},{14,10},{15,11},{22,18},{23,19},{26,22},... | collective-permute-start | bytes 786440 | tf_op jit(solution)/shard_map/ppermute | solution.py:17
  117.5 7.4 %collective-permute-start.14 = (bf16[256,512]{1,0:T(8,128)(2,1)}, bf16[256,512]{1,0:T(8,128)(2,1)}, u32[]{:S(2)}, u32[]{:S(2)}) collective-permute-start(bf16[256,512]{1,0:T(8,128)(2,1)} %get-tuple-element.19), channel_id=1, source_target_pairs={{6,2},{7,3},{10,6},{11,7},{14,10},{15,11},{22,18},{23,19},{26,22},... | collective-permute-start | bytes 786440 | tf_op jit(solution)/shard_map/ppermute | solution.py:17
  119.3 60.4 %collective-permute-start.17 = (bf16[4,128,128]{1,2,0:T(8,128)(2,1)}, bf16[4,128,128]{1,2,0:T(8,128)(2,1)}, u32[]{:S(2)}, u32[]{:S(2)}) collective-permute-start(bf16[4,128,128]{1,2,0:T(8,128)(2,1)} %copy.53), channel_id=1, source_target_pairs={{2,0},{3,1},{4,2},{5,3},{6,4},{7,5},{8,6},{9,7},{10,8},{11,9},{12,... | collective-permute-start | bytes 393224 | tf_op jit(solution)/shard_map/ppermute | solution.py:17
  132.9 22.1 %collective-permute-start.11 = (bf16[256,512]{1,0:T(8,128)(2,1)S(1)}, bf16[256,512]{1,0:T(8,128)(2,1)}, u32[]{:S(2)}, u32[]{:S(2)}) collective-permute-start(bf16[256,512]{1,0:T(8,128)(2,1)S(1)} %fusion.9), channel_id=1, source_target_pairs={{0,1},{4,5},{8,9},{12,13},{6,3},{10,7},{14,11},{16,17},{20,21},{24... | collective-permute-start | bytes 786440 | tf_op jit(solution)/shard_map/ppermute | solution.py:17
  142.4 4.3 %collective-permute-start.10 = (bf16[256,512]{0,1:T(8,128)(2,1)}, bf16[256,512]{0,1:T(8,128)(2,1)S(1)}, u32[]{:S(2)}, u32[]{:S(2)}) collective-permute-start(bf16[256,512]{0,1:T(8,128)(2,1)} %fusion.8), channel_id=1, source_target_pairs={{0,1},{4,5},{8,9},{12,13},{6,3},{10,7},{14,11},{16,17},{20,21},{24... | collective-permute-start | bytes 786440 | tf_op jit(solution)/shard_map/ppermute | solution.py:17
  143.7 11.3 %collective-permute-start.7 = (bf16[256,512]{0,1:T(8,128)(2,1)}, bf16[256,512]{0,1:T(8,128)(2,1)}, u32[]{:S(2)}, u32[]{:S(2)}) collective-permute-start(bf16[256,512]{0,1:T(8,128)(2,1)} %fusion.8), channel_id=1, source_target_pairs={{1,3},{3,1},{5,7},{7,5},{9,11},{11,9},{13,15},{15,13},{17,19},{19,... | collective-permute-start | bytes 786440 | tf_op jit(solution)/shard_map/ppermute | solution.py:17
  145.1 9.9 %collective-permute-start.9 = (bf16[256,512]{0,1:T(8,128)(2,1)S(1)}, bf16[256,512]{0,1:T(8,128)(2,1)}, u32[]{:S(2)}, u32[]{:S(2)}) collective-permute-start(bf16[256,512]{0,1:T(8,128)(2,1)S(1)} %copy.46), channel_id=1, source_target_pairs={{1,3},{3,1},{5,7},{7,5},{9,11},{11,9},{13,15},{15,13},{17,19},{19,... | collective-permute-start | bytes 786440 | tf_op jit(solution)/shard_map/ppermute | solution.py:17
  146.7 33.0 %collective-permute-start.16 = (bf16[4,128,128]{1,2,0:T(8,128)(2,1)}, bf16[4,128,128]{1,2,0:T(8,128)(2,1)}, u32[]{:S(2)}, u32[]{:S(2)}) collective-permute-start(bf16[4,128,128]{1,2,0:T(8,128)(2,1)} %copy.53), channel_id=1, source_target_pairs={{1,0},{2,1},{3,2},{4,3},{5,4},{6,5},{7,6},{8,7},{9,8},{10,9},{11,1... | collective-permute-start | bytes 393224 | tf_op jit(solution)/shard_map/ppermute | solution.py:17
  155.0 8.3 %copy-start.1 = (bf16[512,512]{0,1:T(8,128)(2,1)S(1)}, bf16[512,512]{0,1:T(8,128)(2,1)}, u32[]{:S(2)}) copy-start(bf16[512,512]{0,1:T(8,128)(2,1)} %convolution_multiply_fusion.1) | copy-start | bytes 1572868
  165.0 1.3 copy-start.4
  172.6 12.2 %collective-permute-start.19 = (f32[4,128,128]{1,2,0:T(8,128)}, f32[4,128,128]{1,2,0:T(8,128)S(1)}, u32[]{:S(2)}, u32[]{:S(2)}) collective-permute-start(f32[4,128,128]{1,2,0:T(8,128)} %copy.67), channel_id=1, source_target_pairs={{0,2},{1,3},{2,4},{3,5},{4,6},{5,7},{6,8},{7,9},{8,10},{9,11},{10,... | collective-permute-start | bytes 786440 | tf_op jit(solution)/shard_map/ppermute | solution.py:17
  174.5 11.4 %collective-permute-start.18 = (f32[4,128,128]{1,2,0:T(8,128)}, f32[4,128,128]{1,2,0:T(8,128)S(1)}, u32[]{:S(2)}, u32[]{:S(2)}) collective-permute-start(f32[4,128,128]{1,2,0:T(8,128)} %copy.66), channel_id=1, source_target_pairs={{0,1},{1,2},{2,3},{3,4},{4,5},{5,6},{6,7},{7,8},{8,9},{9,10},{10,1... | collective-permute-start | bytes 786440 | tf_op jit(solution)/shard_map/ppermute | solution.py:17
  176.4 3.3 %copy-start.3 = (f32[4,12]{0,1:T(8,128)S(1)}, f32[4,12]{0,1:T(8,128)}, u32[]{:S(2)}) copy-start(f32[4,12]{0,1:T(8,128)} %copy.50) | copy-start | bytes 580
  176.4 3.3 %copy-start.6 = (pred[4,128]{1,0:T(4,128)(4,1)S(1)}, pred[4,128]{1,0:T(4,128)(4,1)}, u32[]{:S(2)}) copy-start(pred[4,128]{1,0:T(4,128)(4,1)} %iota_compare_fusion.2) | copy-start | bytes 1540

commit v2 on v0

v2 whole, which is shorter than its diff:
```python
import functools
import math

import jax
import jax.numpy as jnp
from jax import lax
from jax.experimental import pallas as pl
from jax.experimental.pallas import tpu as pltpu
from jax.sharding import PartitionSpec as P

REACH = 2
PARTS = 2
BF16 = jnp.bfloat16
F32 = jnp.float32


def gram_kernel(
    devices, factors, sizes, vectors, pairs, gram, sigma,
    own, peer, outer, cross, right, window, acc,
    with_own, with_outer, with_cross, back_two, turned_two, back_one, turned_one,
    terms, got_terms, sums,
    load_sem, send_sem, recv_sem,
):
    rows, depth = own.shape
    half = depth // 2
    count = vectors.shape[0]
    width = rows // count
    slots = (REACH + 1) * count
    step = rows // PARTS
    scale = 1.0 / math.sqrt(depth)
    me = lax.axis_index("atom")
    y = lax.rem(lax.div(me, 2), 2)
    core = lax.rem(me, 2)
    lower, upper = y == 0, y == 1
    even, odd = core == 0, core == 1
    swap = me + 2 - 4 * y
    mate = me + 1 - 2 * core
    kept = pl.multiple_of(y * half, 128)
    given = pl.multiple_of((1 - y) * half, 128)

    used = {}

    def copy(name, source, target, device):
        at = used.setdefault(name, len(used))
        return pltpu.make_async_remote_copy(
            src_ref=source, dst_ref=target, send_sem=send_sem.at[at], recv_sem=recv_sem.at[at],
            device_id={"atom": device}, device_id_type=pl.DeviceIdType.MESH,
        )

    def part(j):
        return pl.ds(j * step, step)

    def load(j):
        return pltpu.make_async_copy(factors.at[part(j)], own.at[part(j)], load_sem.at[j])

    for j in range(PARTS):
        load(j).start()

    barrier = pltpu.get_barrier_semaphore()
    for by in (-4, -3, -2, -1, 1, 2, 3, 4):
        @pl.when((me + by >= 0) & (me + by < devices))
        def _(by=by):
            pl.semaphore_signal(
                barrier, inc=1, device_id={"atom": me + by}, device_id_type=pl.DeviceIdType.MESH
            )
    pl.semaphore_wait(barrier, jnp.minimum(me, 4) + jnp.minimum(devices - 1 - me, 4))

    def peer_copy(j):
        return copy(("peer", j), own.at[part(j), pl.ds(given, half)], peer.at[part(j)], swap)

    far = me - 4 + 8 * y
    far_out = (lower & (me >= 4)) | (upper & (me + 4 < devices))
    far_in = (lower & (me + 4 < devices)) | (upper & (me >= 4))

    def outer_copy(j):
        return copy(("outer", j), own.at[part(j), pl.ds(kept, half)], outer.at[part(j)], far)

    def cross_copy_own(j):
        return copy(("cross", j), own.at[part(j), pl.ds(kept, half)], cross.at[part(j)], mate)

    def cross_copy_outer(j):
        return copy(("cross", j), outer.at[part(j)], cross.at[part(j)], mate)

    def right_copy(j):
        return copy(("right", j), own.at[part(j)], right.at[part(j)], me - 1)

    def window_copy(by):
        return copy(("window", by), vectors, window.at[by - 1], me - by)

    wide = 512
    for j in range(PARTS):
        load(j).wait()

        @pl.loop(0, depth // wide)
        def _(c, j=j):
            at = pl.ds(pl.multiple_of(c * wide, wide), wide)
            for b in range(step // width):
                block = j * (step // width) + b
                lines = pl.ds(block * width, width)
                real = lax.broadcasted_iota(jnp.int32, (width, wide), 0) < sizes[block]
                tile = own[lines, at].astype(F32)
                own[lines, at] = jnp.where(real, tile, 0.0).astype(BF16)

        peer_copy(j).start()
        pl.when(far_out)(lambda j=j: outer_copy(j).start())
        pl.when(y != core)(lambda j=j: cross_copy_own(j).start())
    for j in range(PARTS):
        pl.when(odd)(lambda j=j: right_copy(j).start())
    for by in range(1, REACH + 1):
        pl.when(me >= by)(lambda by=by: window_copy(by).start())

    @pl.when(~far_in)
    def _():
        outer[...] = jnp.zeros_like(outer)

    @pl.when(upper & (me + 4 >= devices))
    def _():
        turned_two[...] = jnp.zeros_like(turned_two)

    @pl.when(odd & upper & (me + 3 >= devices))
    def _():
        turned_one[...] = jnp.zeros_like(turned_one)

    for by in range(1, REACH + 1):
        @pl.when(me + by >= devices)
        def _(by=by):
            window[by - 1] = jnp.zeros_like(window[by - 1])

    def product(left, lines, left_from, other, other_from, length, piece):
        acc[...] = jnp.zeros_like(acc)

        @pl.loop(0, length // piece)
        def _(k):
            a = left[lines, pl.ds(pl.multiple_of(left_from + k * piece, 128), piece)]
            b = other[:, pl.ds(pl.multiple_of(other_from + k * piece, 128), piece)]
            acc[...] += lax.dot_general(a, b, (((1,), (1,)), ((), ())), preferred_element_type=F32)

    piece = half // 3

    def keep_blocks(j, slot):
        for a in range(step // width):
            for b in range(count):
                tile = acc[a * width : (a + 1) * width, b * width : (b + 1) * width] * scale
                gram[j * (step // width) + a, slot * count + b] = tile.astype(BF16)

    for j in range(PARTS):
        product(own, part(j), 0, own, 0, depth, piece)
        keep_blocks(j, 0)

    @pl.when(even)
    def _():
        for j in range(PARTS):
            right_copy(j).wait_recv()
        for j in range(PARTS):
            product(own, part(j), 0, right, 0, depth, piece)
            keep_blocks(j, 1)

    local = pairs[...] - me * count
    code = local[:, 0:1] * slots + local[:, 1:2]
    places = lax.broadcasted_iota(jnp.int32, (pairs.shape[0], 128), 1)
    hot = jnp.where(code == places, 1.0, 0.0).astype(F32)
    apart = jnp.where(local[:, 0:1] != local[:, 1:2], 1.0, 0.0).astype(F32)
    pair_count = jnp.sum(hot, axis=0, keepdims=True)
    cross_count = jnp.sum(hot * apart, axis=0, keepdims=True)

    def two_copy(j, source):
        return copy(("two", j), source.at[part(j)], back_two.at[part(j)], swap)

    def far_copy(j):
        return copy(("far", j), with_outer.at[part(j)], turned_two.at[part(j)], me - 4)

    def one_copy(j):
        return copy(("one", j), with_cross.at[part(j)], back_one.at[part(j)], swap)

    def skew_copy(j):
        return copy(("skew", j), with_cross.at[part(j)], turned_one.at[part(j)], me + 1 - 4 * y)

    for j in range(PARTS):
        @pl.when(far_in)
        def _(j=j):
            outer_copy(j).wait_recv()
        pl.when(y == core)(lambda j=j: cross_copy_outer(j).start())
        peer_copy(j).wait_recv()
        product(peer, part(j), 0, own, kept, half, piece)

        @pl.when(lower)
        def _(j=j):
            turned_two[part(j)] = (acc[...] * scale).astype(BF16)

        @pl.when(upper)
        def _(j=j):
            with_own[part(j)] = (acc[...] * scale).astype(BF16)
            two_copy(j, with_own).start()

    far_back = upper & (me >= 4)
    skew_out = even & (lower | (me >= 3))
    skew_in = odd & (lower | (me + 3 < devices))
    for j in range(PARTS):
        product(peer, part(j), 0, outer, 0, half, piece)
        with_outer[part(j)] = (acc[...] * scale).astype(BF16)
        pl.when(lower)(lambda j=j: two_copy(j, with_outer).start())
        pl.when(far_back)(lambda j=j: far_copy(j).start())
    for j in range(PARTS):
        cross_copy_own(j).wait_recv()
    for j in range(PARTS):
        product(peer, part(j), 0, cross, 0, half, piece)
        with_cross[part(j)] = (acc[...] * scale).astype(BF16)
        pl.when(odd)(lambda j=j: one_copy(j).start())
        pl.when(skew_out)(lambda j=j: skew_copy(j).start())

    for j in range(PARTS):
        two_copy(j, with_own).wait_recv()
        pl.when(upper & (me + 4 < devices))(lambda j=j: far_copy(j).wait_recv())

    def settle(natural, turned, slot):
        for a in range(count):
            for b in range(count):
                ra, rb = slice(a * width, (a + 1) * width), slice(b * width, (b + 1) * width)
                tile = natural[ra, rb].astype(F32) + turned[rb, ra].astype(F32).T
                gram[a, slot * count + b] = tile.astype(BF16)

    settle(back_two, turned_two, 2)

    @pl.when(odd)
    def _():
        for j in range(PARTS):
            one_copy(j).wait_recv()
            pl.when(skew_in)(lambda j=j: skew_copy(j).wait_recv())
        settle(back_one, turned_one, 1)

    for by in range(1, REACH + 1):
        pl.when(me + by < devices)(lambda by=by: window_copy(by).wait_recv())

    def backward(slot):
        total = jnp.zeros((width, vectors.shape[2]), F32)
        for a in range(count):
            term = lax.dot_general(
                gram[a, slot], vectors[a], (((0,), (0,)), ((), ())), preferred_element_type=F32
            )
            at = a * slots + slot
            total = total + term * cross_count[:, at : at + 1]
        return total

    def terms_copy(by):
        return copy(("terms", by), terms.at[by - 1], got_terms.at[by - 1], me + by)

    for by in range(REACH, 0, -1):
        for b in range(count):
            terms[by - 1, b] = backward(by * count + b).astype(BF16)
        pl.when(me + by < devices)(lambda by=by: terms_copy(by).start())

    totals = []
    for a in range(count):
        total = backward(a)
        for slot in range(slots):
            column = vectors[slot] if slot < count else window[slot // count - 1, slot % count]
            at = a * slots + slot
            term = jnp.dot(gram[a, slot], column, preferred_element_type=F32)
            total = total + term * pair_count[:, at : at + 1]
        sums[a * width : (a + 1) * width] = total
    for by in range(1, REACH + 1):
        @pl.when(me >= by)
        def _(by=by):
            terms_copy(by).wait_recv()
            for a in range(count):
                lines = slice(a * width, (a + 1) * width)
                sums[lines] += got_terms[by - 1, a].astype(F32)
    for a in range(count):
        sigma[a] = sums[a * width : (a + 1) * width].astype(BF16)

    for j in range(PARTS):
        peer_copy(j).wait_send()
        pl.when(far_out)(lambda j=j: outer_copy(j).wait_send())
        cross_copy_own(j).wait_send()
        pl.when(odd)(lambda j=j: right_copy(j).wait_send())
        two_copy(j, with_own).wait_send()
        pl.when(far_back)(lambda j=j: far_copy(j).wait_send())
        pl.when(odd)(lambda j=j: one_copy(j).wait_send())
        pl.when(skew_out)(lambda j=j: skew_copy(j).wait_send())
    for by in range(1, REACH + 1):
        pl.when(me >= by)(lambda by=by: window_copy(by).wait_send())
        pl.when(me + by < devices)(lambda by=by: terms_copy(by).wait_send())


def pick_kernel(pairs, gram, kblocks, sem):
    count, slots = gram.shape[0], gram.shape[1]
    npairs = kblocks.shape[0]
    start = lax.axis_index("atom") * count

    @pl.loop(0, npairs)
    def _(p):
        pltpu.make_async_copy(
            gram.at[pairs[p, 0] - start, pairs[p, 1] - start], kblocks.at[p], sem
        ).start()

    pltpu.make_async_copy(kblocks, kblocks, sem).wait()


def on_device(factors, block_sizes, trial_vectors, pair_list):
    count, width, depth = factors.shape
    rows = count * width
    half = depth // 2
    slots = (REACH + 1) * count
    devices = lax.axis_size("atom")
    copies = 8 * PARTS + 2 * REACH
    vmem, smem, hbm = pltpu.VMEM, pltpu.SMEM, pl.ANY
    nvec = trial_vectors.shape[2]
    gram, sigma = pl.pallas_call(
        functools.partial(gram_kernel, devices),
        out_shape=(
            jax.ShapeDtypeStruct((count, slots, width, width), BF16),
            jax.ShapeDtypeStruct(trial_vectors.shape, BF16),
        ),
        in_specs=[pl.BlockSpec(memory_space=s) for s in (hbm, smem, vmem, vmem)],
        out_specs=(pl.BlockSpec(memory_space=vmem), pl.BlockSpec(memory_space=vmem)),
        scratch_shapes=[
            pltpu.VMEM((rows, depth), BF16),
            pltpu.VMEM((rows, half), BF16),
            pltpu.VMEM((rows, half), BF16),
            pltpu.VMEM((rows, half), BF16),
            pltpu.VMEM((rows, depth), BF16),
            pltpu.VMEM((REACH, count, width, nvec), BF16),
            pltpu.VMEM((rows // PARTS, rows), F32),
        ]
        + [pltpu.VMEM((rows, rows), BF16)] * 7
        + [
            pltpu.VMEM((REACH, count, width, nvec), BF16),
            pltpu.VMEM((REACH, count, width, nvec), BF16),
            pltpu.VMEM((rows, nvec), F32),
            pltpu.SemaphoreType.DMA((PARTS,)),
            pltpu.SemaphoreType.DMA((copies,)),
            pltpu.SemaphoreType.DMA((copies,)),
        ],
        compiler_params=pltpu.CompilerParams(
            collective_id=0, has_side_effects=True, vmem_limit_bytes=56 * 1024 * 1024
        ),
    )(factors.reshape(rows, depth), block_sizes, trial_vectors, pair_list)
    kblocks = pl.pallas_call(
        pick_kernel,
        out_shape=jax.ShapeDtypeStruct((pair_list.shape[0], width, width), BF16),
        in_specs=[pl.BlockSpec(memory_space=smem), pl.BlockSpec(memory_space=vmem)],
        out_specs=pl.BlockSpec(memory_space=hbm),
        scratch_shapes=[pltpu.SemaphoreType.DMA],
        compiler_params=pltpu.CompilerParams(vmem_limit_bytes=32 * 1024 * 1024),
    )(pair_list, gram)
    return (kblocks, sigma)


def solution(mesh):
    return jax.shard_map(
        on_device,
        mesh=mesh,
        in_specs=(
            P(("groups", "atom"), None, None),
            P(("groups", "atom")),
            P(("groups", "atom"), None, None),
            P(("groups", "atom"), None),
        ),
        out_specs=(P(("groups", "atom"), None, None), P(("groups", "atom"), None, None)),
        check_vma=False,
    )
```

time: 254 us -> 109 us (0.43)
  waiting for transfers between devices: 199 us -> 0 us
  Pallas kernels: 0 us -> 105 us
  matrix products: 19.9 us -> 0 us
  starting transfers between devices: 15.3 us -> 0 us
  other arithmetic: 7.88 us -> 0 us
  local copies, waits for them, and re-layouts: 9.01 us -> 3.45 us
    ppermute x6 -> x0, waiting for transfers between devices: 199 us -> none  [passed_along(): return lax.ppermute(value, axis, pairs)]
    pallas_call x0 -> x2, Pallas kernels: none -> 105 us  [the longest x1 102 us: on_device(): pl.pallas_call(functools.partial(gram_kernel, devices), out_shape=(jax.Sh...]
    dot_general x4 -> x0, matrix products: 19.9 us -> none  [the longest x1 14.8 us: on_device(): jnp.einsum('aiq,bjq->abij', masked, window_factors, preferred_element_typ...]
    ppermute x6 -> x0, starting transfers between devices: 15.3 us -> none  [passed_along(): return lax.ppermute(value, axis, pairs)]
    mul x1 -> x0, other arithmetic: 5.93 us -> none  [on_device(): masked = factors * keep[:, :, None]]
    unnamed x18 -> x8, local copies, waits for them, and re-layouts: 6.56 us -> 3.45 us
  transfers between devices with their start and end apart: 6 -> 0, of which waited for: 3 -> 0; matrix products, arithmetic and copies ran while one was open for 11% -> 0% of each run, Pallas kernels for 0% -> 0%
where the time goes in v2:
time: 109 us
  Pallas kernels  105 us (96%)
  local copies, waits for them, and re-layouts  3.45 us (3%)
    pallas_call x1, Pallas kernels, on_device(): pl.pallas_call(functools.partial(gram_kernel, devices), out_shape=(jax.Sh...  102 us
    unnamed x8, local copies, waits for them, and re-layouts  3.45 us
    pallas_call x1, Pallas kernels, on_device(): pl.pallas_call(pick_kernel, out_shape=jax.ShapeDtypeStruct((pair_list.sha...  2.37 us

profile of v2, /device:TPU:8, one launch (start us, length us, event | category | flops | bytes accessed | tf_op | source)
XLA Modules:
  0.0 108.8 jit_solution(551622044570941090)
XLA Ops:
  0.6 1.4 %copy.7.pairs = s32[64,2]{1,0:T(8,128)} copy(s32[64,2]{0,1:T(2,128)} %param.7) | data formatting | bytes 1024 | tf_op args[3]
  2.0 0.0 copy-start.1
  2.0 102.3 %shard_map.59 = (bf16[4,12,128,128]{3,2,1,0:T(8,128)(2,1)}, bf16[4,128,128]{2,1,0:T(8,128)(2,1)}) custom-call(bf16[512,6144]{1,0:T(8,128)(2,1)} %bitcast.1, s32[4]{0:T(128)} %sizes.1, bf16[4,128,128]{2,1,0:T(8,128)(2,1)} %vectors.1, s32[64,2]{1,0:T(8,128)} %copy.7.pairs), custom_call_target="tpu_custom_call" | custom-call | tf_op jit(solution)/shard_map/pallas_call | solution.py:308
  104.4 0.0 copy-done.1
  104.4 0.0 copy-start
  104.4 1.4 %copy-done = bf16[4,12,128,128]{3,2,1,0:T(8,128)(2,1)S(1)} copy-done((bf16[4,12,128,128]{3,2,1,0:T(8,128)(2,1)S(1)}, bf16[4,12,128,128]{3,2,1,0:T(8,128)(2,1)}, u32[]{:S(2)}) %copy-start) | copy-done | bytes 1572888
  105.8 0.0 copy-start.2
  105.8 2.4 %shard_map.60 = bf16[64,128,128]{2,1,0:T(8,128)(2,1)} custom-call(s32[64,2]{1,0:T(8,128)S(1)} %copy-done.1, bf16[4,12,128,128]{3,2,1,0:T(8,128)(2,1)S(1)} %copy-done), custom_call_target="tpu_custom_call" | custom-call | tf_op jit(solution)/shard_map/pallas_call | solution.py:338
  108.2 0.0 copy-done.2
  108.2 0.7 copy.9
Async XLA Ops:
  2.0 102.3 %copy-start.1 = (s32[64,2]{1,0:T(8,128)S(1)}, s32[64,2]{1,0:T(8,128)}, u32[]{:S(2)}) copy-start(s32[64,2]{1,0:T(8,128)} %copy.7.pairs) | copy-start | bytes 1540
  104.4 1.4 %copy-start = (bf16[4,12,128,128]{3,2,1,0:T(8,128)(2,1)S(1)}, bf16[4,12,128,128]{3,2,1,0:T(8,128)(2,1)}, u32[]{:S(2)}) copy-start(bf16[4,12,128,128]{3,2,1,0:T(8,128)(2,1)} %get-tuple-element.4.gram) | copy-start | bytes 4718596
  105.8 2.4 %copy-start.2 = (bf16[4,128,128]{2,1,0:T(8,128)(2,1)S(1)}, bf16[4,128,128]{2,1,0:T(8,128)(2,1)}, u32[]{:S(2)}) copy-start(bf16[4,128,128]{2,1,0:T(8,128)(2,1)} %get-tuple-element.9) | copy-start | bytes 393220

commit v3 on v2

v3 whole, which is shorter than its diff:
```python
import functools
import math

import jax
import jax.numpy as jnp
from jax import lax
from jax.experimental import pallas as pl
from jax.experimental.pallas import tpu as pltpu
from jax.sharding import PartitionSpec as P

REACH = 2
PARTS = 2
BF16 = jnp.bfloat16
F32 = jnp.float32


def gram_kernel(
    devices, factors, sizes, vectors, pairs, pairs_at, kblocks, sigma,
    gram, picked, mark, window_mark,
    own, peer, outer, cross, right, window, acc,
    with_own, with_outer, with_cross, back_two, turned_two, back_one, turned_one,
    terms, got_terms, sums,
    load_sem, out_sem, send_sem, recv_sem,
):
    rows, depth = own.shape
    half = depth // 2
    count = vectors.shape[0]
    width = rows // count
    slots = (REACH + 1) * count
    step = rows // PARTS
    scale = 1.0 / math.sqrt(depth)
    me = lax.axis_index("atom")
    y = lax.rem(lax.div(me, 2), 2)
    core = lax.rem(me, 2)
    lower, upper = y == 0, y == 1
    even, odd = core == 0, core == 1
    swap = me + 2 - 4 * y
    mate = me + 1 - 2 * core
    kept = pl.multiple_of(y * half, 128)
    given = pl.multiple_of((1 - y) * half, 128)

    used = {}

    def copy(name, source, target, device):
        at = used.setdefault(name, len(used))
        return pltpu.make_async_remote_copy(
            src_ref=source, dst_ref=target, send_sem=send_sem.at[at], recv_sem=recv_sem.at[at],
            device_id={"atom": device}, device_id_type=pl.DeviceIdType.MESH,
        )

    def part(j):
        return pl.ds(j * step, step)

    def load(j):
        return pltpu.make_async_copy(factors.at[part(j)], own.at[part(j)], load_sem.at[j])

    for j in range(PARTS):
        load(j).start()

    barrier = pltpu.get_barrier_semaphore()
    for by in (-4, -3, -2, -1, 1, 2, 3, 4):
        @pl.when((me + by >= 0) & (me + by < devices))
        def _(by=by):
            pl.semaphore_signal(
                barrier, inc=1, device_id={"atom": me + by}, device_id_type=pl.DeviceIdType.MESH
            )
    pl.semaphore_wait(barrier, jnp.minimum(me, 4) + jnp.minimum(devices - 1 - me, 4))

    def peer_copy(j):
        return copy(("peer", j), factors.at[part(j), pl.ds(given, half)], peer.at[part(j)], swap)

    far = me - 4 + 8 * y
    far_out = (lower & (me >= 4)) | (upper & (me + 4 < devices))
    far_in = (lower & (me + 4 < devices)) | (upper & (me >= 4))

    def outer_copy(j):
        return copy(("outer", j), factors.at[part(j), pl.ds(kept, half)], outer.at[part(j)], far)

    def cross_copy_own(j):
        return copy(("cross", j), factors.at[part(j), pl.ds(kept, half)], cross.at[part(j)], mate)

    def cross_copy_outer(j):
        return copy(("cross", j), outer.at[part(j)], cross.at[part(j)], mate)

    def right_copy(j):
        return copy(("right", j), factors.at[part(j)], right.at[part(j)], me - 1)

    def window_copy(by, source=vectors):
        return copy(("window", by), source, window.at[by - 1], me - 2 if by == 2 else mate)

    def mark_copy(by):
        return copy(("mark", by), mark, window_mark.at[by - 1], me - by)

    for b in range(count):
        real = lax.broadcasted_iota(jnp.int32, mark.shape[1:], 1) < sizes[b]
        mark[b] = jnp.where(real, 1.0, 0.0).astype(BF16)
    for j in range(PARTS):
        peer_copy(j).start()
        pl.when(far_out)(lambda j=j: outer_copy(j).start())
        pl.when(y != core)(lambda j=j: cross_copy_own(j).start())
        if j == 0:
            for by in range(1, REACH + 1):
                pl.when(me >= by)(lambda by=by: mark_copy(by).start())
    for j in range(PARTS):
        pl.when(odd)(lambda j=j: right_copy(j).start())
    for by in range(1, REACH + 1):
        pl.when(me >= 2 if by == 2 else odd)(lambda by=by: window_copy(by).start())

    @pl.when(~far_in)
    def _():
        outer[...] = jnp.zeros_like(outer)

    @pl.when(upper & (me + 4 >= devices))
    def _():
        turned_two[...] = jnp.zeros_like(turned_two)

    @pl.when(odd & upper & (me + 3 >= devices))
    def _():
        turned_one[...] = jnp.zeros_like(turned_one)

    for by in range(1, REACH + 1):
        @pl.when(me + by >= devices)
        def _(by=by):
            window[by - 1] = jnp.zeros_like(window[by - 1])
            window_mark[by - 1] = jnp.zeros_like(window_mark[by - 1])

    for j in range(PARTS):
        load(j).wait()

    def product(left, lines, left_from, other, other_from, length, piece):
        acc[...] = jnp.zeros_like(acc)

        @pl.loop(0, length // piece)
        def _(k):
            a = left[lines, pl.ds(pl.multiple_of(left_from + k * piece, 128), piece)]
            b = other[:, pl.ds(pl.multiple_of(other_from + k * piece, 128), piece)]
            acc[...] += lax.dot_general(a, b, (((1,), (1,)), ((), ())), preferred_element_type=F32)

    piece = half // 3

    def real_only(tile, a, slot, b):
        lines = lax.broadcasted_iota(jnp.int32, (width, width), 0) < sizes[a]
        columns = mark[b, 0:1] if slot == 0 else window_mark[slot - 1, b, 0:1]
        return (jnp.where(lines, tile, 0.0) * columns.astype(F32)).astype(BF16)

    def keep_blocks(j, slot):
        for a in range(step // width):
            for b in range(count):
                tile = acc[a * width : (a + 1) * width, b * width : (b + 1) * width] * scale
                at = j * (step // width) + a
                gram[at, slot * count + b] = real_only(tile, at, slot, b)

    for j in range(PARTS):
        product(own, part(j), 0, own, 0, depth, piece)
        keep_blocks(j, 0)

    for by in range(1, REACH + 1):
        pl.when(me + by < devices)(lambda by=by: mark_copy(by).wait_recv())

    @pl.when(even)
    def _():
        for j in range(PARTS):
            right_copy(j).wait_recv()
        for j in range(PARTS):
            product(own, part(j), 0, right, 0, depth, piece)
            keep_blocks(j, 1)

    local = pairs[...] - me * count
    code = local[0:1] * slots + local[1:2]
    places = lax.broadcasted_iota(jnp.int32, (count * slots, pairs.shape[1]), 0)
    hot = jnp.where(code == places, 1.0, 0.0).astype(F32)
    apart = jnp.where(local[0:1] != local[1:2], 1.0, 0.0).astype(F32)
    pair_count = jnp.sum(hot, axis=1, keepdims=True)
    cross_count = jnp.sum(hot * apart, axis=1, keepdims=True)

    def two_copy(j, source):
        return copy(("two", j), source.at[part(j)], back_two.at[part(j)], swap)

    def far_copy(j):
        return copy(("far", j), with_outer.at[part(j)], turned_two.at[part(j)], me - 4)

    def one_copy(j):
        return copy(("one", j), with_cross.at[part(j)], back_one.at[part(j)], swap)

    def skew_copy(j):
        return copy(("skew", j), with_cross.at[part(j)], turned_one.at[part(j)], me + 1 - 4 * y)

    def turn_own(j):
        product(peer, part(j), 0, own, kept, half, piece)
        turned_two[part(j)] = (acc[...] * scale).astype(BF16)

    for j in range(PARTS):
        @pl.when(far_in)
        def _(j=j):
            outer_copy(j).wait_recv()
        pl.when(y == core)(lambda j=j: cross_copy_outer(j).start())
        peer_copy(j).wait_recv()

        @pl.when(upper)
        def _(j=j):
            product(peer, part(j), 0, own, kept, half, piece)
            with_own[part(j)] = (acc[...] * scale).astype(BF16)
            two_copy(j, with_own).start()

        if j < PARTS - 1:
            pl.when(lower)(lambda j=j: turn_own(j))

    far_back = upper & (me >= 4)
    skew_out = even & (lower | (me >= 3))
    skew_in = odd & (lower | (me + 3 < devices))
    @pl.when(lower)
    def _():
        for j in range(PARTS):
            product(peer, part(j), 0, outer, 0, half, piece)
            with_outer[part(j)] = (acc[...] * scale).astype(BF16)
            two_copy(j, with_outer).start()

    for j in range(PARTS):
        cross_copy_own(j).wait_recv()
    for j in range(PARTS):
        product(peer, part(j), 0, cross, 0, half, piece)
        with_cross[part(j)] = (acc[...] * scale).astype(BF16)
        pl.when(odd)(lambda j=j: one_copy(j).start())
        pl.when(skew_out)(lambda j=j: skew_copy(j).start())
    pl.when(lower)(lambda: turn_own(PARTS - 1))

    @pl.when(far_back)
    def _():
        for j in range(PARTS):
            product(peer, part(j), 0, outer, 0, half, piece)
            with_outer[part(j)] = (acc[...] * scale).astype(BF16)
            far_copy(j).start()

    passing = even & (me + 2 < devices)

    @pl.when(me + 2 < devices)
    def _():
        window_copy(2).wait_recv()

        @pl.when(even)
        def _():
            window_copy(1, window.at[1]).start()

    for j in range(PARTS):
        two_copy(j, with_own).wait_recv()
        pl.when(upper & (me + 4 < devices))(lambda j=j: far_copy(j).wait_recv())

    def settle(natural, turned, slot):
        for a in range(count):
            for b in range(count):
                ra, rb = slice(a * width, (a + 1) * width), slice(b * width, (b + 1) * width)
                tile = natural[ra, rb].astype(F32) + turned[rb, ra].astype(F32).T
                gram[a, slot * count + b] = real_only(tile, a, slot, b)

    def backward(slot):
        total = jnp.zeros((width, vectors.shape[2]), F32)
        for a in range(count):
            term = lax.dot_general(
                gram[a, slot], vectors[a], (((0,), (0,)), ((), ())), preferred_element_type=F32
            )
            at = a * slots + slot
            total = total + term * cross_count[at : at + 1]
        return total

    def terms_copy(by):
        return copy(("terms", by), terms.at[by - 1], got_terms.at[by - 1], me + by)

    def leave(by):
        for b in range(count):
            terms[by - 1, b] = backward(by * count + b).astype(BF16)
        pl.when(me + by < devices)(lambda: terms_copy(by).start())

    settle(back_two, turned_two, 2)

    leave(2)

    @pl.when(odd)
    def _():
        for j in range(PARTS):
            one_copy(j).wait_recv()
            pl.when(skew_in)(lambda j=j: skew_copy(j).wait_recv())
        settle(back_one, turned_one, 1)

    leave(1)

    @pl.loop(0, picked.shape[0])
    def _(p):
        a = jnp.clip(pairs_at[0, p] - me * count, 0, count - 1)
        b = jnp.clip(pairs_at[1, p] - me * count, 0, slots - 1)
        picked[p] = gram[a, b]

    result = pltpu.make_async_copy(picked, kblocks, out_sem)
    result.start()
    pl.when(me + 1 < devices)(lambda: window_copy(1).wait_recv())

    for a in range(count):
        total = backward(a)
        for slot in range(slots):
            column = vectors[slot] if slot < count else window[slot // count - 1, slot % count]
            at = a * slots + slot
            term = jnp.dot(gram[a, slot], column, preferred_element_type=F32)
            total = total + term * pair_count[at : at + 1]
        sums[a * width : (a + 1) * width] = total
    for by in range(1, REACH + 1):
        @pl.when(me >= by)
        def _(by=by):
            terms_copy(by).wait_recv()
            for a in range(count):
                lines = slice(a * width, (a + 1) * width)
                sums[lines] += got_terms[by - 1, a].astype(F32)
    for a in range(count):
        sigma[a] = sums[a * width : (a + 1) * width].astype(BF16)

    result.wait()
    for j in range(PARTS):
        peer_copy(j).wait_send()
        pl.when(far_out)(lambda j=j: outer_copy(j).wait_send())
        cross_copy_own(j).wait_send()
        pl.when(odd)(lambda j=j: right_copy(j).wait_send())
        two_copy(j, with_own).wait_send()
        pl.when(far_back)(lambda j=j: far_copy(j).wait_send())
        pl.when(odd)(lambda j=j: one_copy(j).wait_send())
        pl.when(skew_out)(lambda j=j: skew_copy(j).wait_send())
    for by in range(1, REACH + 1):
        pl.when(me >= 2 if by == 2 else odd | passing)(lambda by=by: window_copy(by).wait_send())
        pl.when(me >= by)(lambda by=by: mark_copy(by).wait_send())
        pl.when(me + by < devices)(lambda by=by: terms_copy(by).wait_send())


def on_device(factors, block_sizes, trial_vectors, pair_list):
    count, width, depth = factors.shape
    rows = count * width
    half = depth // 2
    slots = (REACH + 1) * count
    devices = lax.axis_size("atom")
    copies = 8 * PARTS + 3 * REACH
    vmem, smem, hbm = pltpu.VMEM, pltpu.SMEM, pl.ANY
    nvec = trial_vectors.shape[2]
    npairs = pair_list.shape[0]
    turned_list = pair_list.T
    return pl.pallas_call(
        functools.partial(gram_kernel, devices),
        out_shape=(
            jax.ShapeDtypeStruct((npairs, width, width), BF16),
            jax.ShapeDtypeStruct(trial_vectors.shape, BF16),
        ),
        in_specs=[pl.BlockSpec(memory_space=s) for s in (hbm, smem, vmem, vmem, smem)],
        out_specs=(pl.BlockSpec(memory_space=hbm), pl.BlockSpec(memory_space=vmem)),
        scratch_shapes=[
            pltpu.VMEM((count, slots, width, width), BF16),
            pltpu.VMEM((npairs, width, width), BF16),
            pltpu.VMEM((count, 16, width), BF16),
            pltpu.VMEM((REACH, count, 16, width), BF16),
            pltpu.VMEM((rows, depth), BF16),
            pltpu.VMEM((rows, half), BF16),
            pltpu.VMEM((rows, half), BF16),
            pltpu.VMEM((rows, half), BF16),
            pltpu.VMEM((rows, depth), BF16),
            pltpu.VMEM((REACH, count, width, nvec), BF16),
            pltpu.VMEM((rows // PARTS, rows), F32),
        ]
        + [pltpu.VMEM((rows, rows), BF16)] * 7
        + [
            pltpu.VMEM((REACH, count, width, nvec), BF16),
            pltpu.VMEM((REACH, count, width, nvec), BF16),
            pltpu.VMEM((rows, nvec), F32),
            pltpu.SemaphoreType.DMA((PARTS,)),
            pltpu.SemaphoreType.DMA,
            pltpu.SemaphoreType.DMA((copies,)),
            pltpu.SemaphoreType.DMA((copies,)),
        ],
        compiler_params=pltpu.CompilerParams(
            collective_id=0, has_side_effects=True, vmem_limit_bytes=56 * 1024 * 1024
        ),
    )(factors.reshape(rows, depth), block_sizes, trial_vectors, turned_list, turned_list)


def solution(mesh):
    return jax.shard_map(
        on_device,
        mesh=mesh,
        in_specs=(
            P(("groups", "atom"), None, None),
            P(("groups", "atom")),
            P(("groups", "atom"), None, None),
            P(("groups", "atom"), None),
        ),
        out_specs=(P(("groups", "atom"), None, None), P(("groups", "atom"), None, None)),
        check_vma=False,
    )
```

time: 109 us -> 106 us (0.972)
  Pallas kernels: 105 us -> 102 us
    pallas_call x1 -> x0, Pallas kernels: 2.37 us -> none  [on_device(): pl.pallas_call(pick_kernel, out_shape=jax.ShapeDtypeStruct((pair_list.sha...]
    unnamed x8 -> x4, local copies, waits for them, and re-layouts: 3.45 us -> 3.85 us
where the time goes in v3:
time: 106 us
  Pallas kernels  102 us (96%)
  local copies, waits for them, and re-layouts  3.85 us (4%)
    pallas_call x1, Pallas kernels, on_device(): pl.pallas_call(functools.partial(gram_kernel, devices), out_shape=(jax.Sh...  102 us
    unnamed x4, local copies, waits for them, and re-layouts  3.85 us

profile of v3, /device:TPU:8, one launch (start us, length us, event | category | flops | bytes accessed | tf_op | source)
XLA Modules:
  0.0 106.2 jit_solution(2078360091659617482)
XLA Ops:
  0.6 101.7 %shard_map.59 = (bf16[64,128,128]{2,1,0:T(8,128)(2,1)}, bf16[4,128,128]{2,1,0:T(8,128)(2,1)}) custom-call(bf16[512,6144]{1,0:T(8,128)(2,1)} %bitcast.2, s32[4]{0:T(128)} %sizes.1, bf16[4,128,128]{2,1,0:T(8,128)(2,1)} %vectors.1, s32[2,64]{1,0:T(2,128)} %bitcast.3, s32[2,64]{1,0:T(2,128)} %bitcast.4), custom_call_target="tpu_custom_call" | custom-call | tf_op jit(solution)/shard_map/pallas_call | solution.py:341
  102.4 0.0 copy-start
  102.4 3.2 %copy.8 = bf16[64,128,128]{2,1,0:T(8,128)(2,1)} copy(bf16[64,128,128]{2,1,0:T(8,128)(2,1)} %get-tuple-element.4) | data formatting | bytes 4194304
  105.6 0.0 copy-done
  105.6 0.7 copy.9
Async XLA Ops:
  102.4 3.2 %copy-start = (bf16[4,128,128]{2,1,0:T(8,128)(2,1)S(1)}, bf16[4,128,128]{2,1,0:T(8,128)(2,1)}, u32[]{:S(2)}) copy-start(bf16[4,128,128]{2,1,0:T(8,128)(2,1)} %get-tuple-element.5) | copy-start | bytes 393220

commit v4 on v3

--- a/solution.py
+++ b/solution.py
@@ -10,6 +10,7 @@
 
 REACH = 2
 PARTS = 2
+GROUP = 8
 BF16 = jnp.bfloat16
 F32 = jnp.float32
 
@@ -327,6 +328,29 @@
         pl.when(me + by < devices)(lambda by=by: terms_copy(by).wait_send())
 
 
+def hand_on_kernel(blocks, sigma, blocks_out, sigma_out, held, held_sigma, in_sem, out_sem):
+    pieces = held.shape[0] // GROUP
+    def into(j):
+        if j == pieces:
+            return pltpu.make_async_copy(sigma, held_sigma, in_sem.at[j])
+        at = pl.ds(j * GROUP, GROUP)
+        return pltpu.make_async_copy(blocks.at[at], held.at[at], in_sem.at[j])
+
+    def out(j):
+        if j == pieces:
+            return pltpu.make_async_copy(held_sigma, sigma_out, out_sem.at[j])
+        at = pl.ds(j * GROUP, GROUP)
+        return pltpu.make_async_copy(held.at[at], blocks_out.at[at], out_sem.at[j])
+
+    for j in range(pieces + 1):
+        into(j).start()
+    for j in range(pieces + 1):
+        into(j).wait()
+        out(j).start()
+    for j in range(pieces + 1):
+        out(j).wait()
+
+
 def on_device(factors, block_sizes, trial_vectors, pair_list):
     count, width, depth = factors.shape
     rows = count * width
@@ -338,7 +362,7 @@
     nvec = trial_vectors.shape[2]
     npairs = pair_list.shape[0]
     turned_list = pair_list.T
-    return pl.pallas_call(
+    blocks, sigma = pl.pallas_call(
         functools.partial(gram_kernel, devices),
         out_shape=(
             jax.ShapeDtypeStruct((npairs, width, width), BF16),
@@ -373,6 +397,21 @@
             collective_id=0, has_side_effects=True, vmem_limit_bytes=56 * 1024 * 1024
         ),
     )(factors.reshape(rows, depth), block_sizes, trial_vectors, turned_list, turned_list)
+    return pl.pallas_call(
+        hand_on_kernel,
+        out_shape=(
+            jax.ShapeDtypeStruct(blocks.shape, BF16),
+            jax.ShapeDtypeStruct(sigma.shape, BF16),
+        ),
+        in_specs=[pl.BlockSpec(memory_space=hbm)] * 2,
+        out_specs=(pl.BlockSpec(memory_space=hbm), pl.BlockSpec(memory_space=hbm)),
+        scratch_shapes=[
+            pltpu.VMEM(blocks.shape, BF16),
+            pltpu.VMEM(sigma.shape, BF16),
+            pltpu.SemaphoreType.DMA((npairs // GROUP + 1,)),
+            pltpu.SemaphoreType.DMA((npairs // GROUP + 1,)),
+        ],
+    )(blocks, sigma)
 
 
 def solution(mesh):

time: 106 us -> 105 us (level)
  local copies, waits for them, and re-layouts: 3.85 us -> 0 us
  Pallas kernels: 102 us -> 104 us
    unnamed x4 -> x0, local copies, waits for them, and re-layouts: 3.85 us -> none
    pallas_call x0 -> x1, Pallas kernels: none -> 2.45 us  [on_device(): pl.pallas_call(hand_on_kernel, out_shape=(jax.ShapeDtypeStruct(blocks.sha...]
where the time goes in v4:
time: 105 us
  Pallas kernels  104 us (99%)
    pallas_call x1, Pallas kernels, on_device(): pl.pallas_call(functools.partial(gram_kernel, devices), out_shape=(jax.Sh...  102 us
    pallas_call x1, Pallas kernels, on_device(): pl.pallas_call(hand_on_kernel, out_shape=(jax.ShapeDtypeStruct(blocks.sha...  2.45 us

profile of v4, /device:TPU:8, one launch (start us, length us, event | category | flops | bytes accessed | tf_op | source)
XLA Modules:
  0.0 104.8 jit_solution(10853754253766767661)
XLA Ops:
  0.6 101.7 %shard_map.59 = (bf16[64,128,128]{2,1,0:T(8,128)(2,1)}, bf16[4,128,128]{2,1,0:T(8,128)(2,1)}) custom-call(bf16[512,6144]{1,0:T(8,128)(2,1)} %bitcast.2, s32[4]{0:T(128)} %sizes.1, bf16[4,128,128]{2,1,0:T(8,128)(2,1)} %vectors.1, s32[2,64]{1,0:T(2,128)} %bitcast.3, s32[2,64]{1,0:T(2,128)} %bitcast.4), custom_call_target="tpu_custom_call" | custom-call | tf_op jit(solution)/shard_map/pallas_call | solution.py:365
  102.4 2.5 %shard_map.60 = (bf16[64,128,128]{2,1,0:T(8,128)(2,1)}, bf16[4,128,128]{2,1,0:T(8,128)(2,1)}) custom-call(bf16[64,128,128]{2,1,0:T(8,128)(2,1)} %get-tuple-element.4.blocks, bf16[4,128,128]{2,1,0:T(8,128)(2,1)} %get-tuple-element.5.sigma), custom_call_target="tpu_custom_call" | custom-call | tf_op jit(solution)/shard_map/pallas_call | solution.py:400
